TPU v7x, 768 devices: a whole 4x8x12 slice. The times are simulated.
768 devices in a mesh: replica: 4 (over x_lo, core), shard: 192 (over x_hi, z, y).
Axes of the slice: x: 4 (x_hi: 2, x_lo: 2; x = x_hi * 2 + x_lo), y: 8, z: 12, core: 2. Of those that a mesh axis runs over, the one named last changes fastest.
Arguments:
- inner_params: bfloat16 [4, 15360, 4096], P('replica', 'shard'), may hold values from -6 to 6
- anchor: float32 [15360, 4096], P('shard'), may hold values from -6 to 6
- momentum: float32 [15360, 4096], P('shard'), may hold values from -2 to 2
- first_moment: bfloat16 [4, 15360, 4096], P('replica', 'shard'), may hold values from -0.59765625 to 0.59765625
- second_moment: bfloat16 [4, 15360, 4096], P('replica', 'shard'), may hold values from 0.0009994507 to 0.099609375
- activations: bfloat16 [4, 768, 4096], P('replica', 'shard'), may hold values from -6 to 6
- cotangent: bfloat16 [4, 15360, 768], P('replica', 'shard'), may hold values from -6 to 6
- spare_index: int32 [192], P('shard'), may hold values from 0 to 3
- peer_index: int32 [192], P('shard'), may hold values from 0 to 3
Outputs:
- anchor_new: float32 [15360, 4096], P('shard')
- momentum_new: float32 [15360, 4096], P('shard')
- update: float32 [4, 15360, 4096], P('replica', 'shard')
Inputs may be any that keep to these rules, and one draw needn't show every extreme that they name: `spare_index`: a replica index for each block. `peer_index`: a replica index for each block; where it equals spare_index the spare keeps its own moments.
All inputs are finite; a program needn't handle non-finite values.
Results may differ from a plain program's by a relative error of at most 0.0018.
Values may be sent and summed in bfloat16 or wider, within the bound.
A program may use at most 64 MiB of HBM per device.

v0:
```python
import math

import jax
import jax.numpy as jnp
from jax import lax
from jax.sharding import PartitionSpec as P

outer_rate = 0.7
nesterov_mu = 0.9
beta_one = 0.9
beta_two = 0.95
bias_one = 1.0 - 0.9**40
bias_two = 1.0 - 0.95**40
adam_eps = 1e-08
decay_rate = 0.1


def from_root(block, axis, holder):
    block = jnp.where(lax.axis_index(axis) == holder, block, jnp.zeros_like(block))
    return lax.psum(block, axis)


def slope(pre):
    sigma = jax.nn.sigmoid(pre)
    return sigma * (1.0 + pre * (1.0 - sigma))


def local(
    inner_params,
    anchor,
    momentum,
    first_moment,
    second_moment,
    activations,
    cotangent,
    spare_index,
    peer_index,
):
    replicas = lax.axis_size("replica")
    position = lax.axis_index("replica")
    spare_slot = spare_index[0]
    peer_slot = peer_index[0]
    healthy = (position != spare_slot).astype(jnp.float32)
    difference = (anchor - inner_params[0].astype(jnp.float32)) * healthy
    summed = lax.psum(difference, "replica")
    average = summed / (replicas - 1)
    momentum_new = nesterov_mu * momentum + average
    anchor_new = anchor - outer_rate * (average + nesterov_mu * momentum_new)
    received = (
        from_root(first_moment, "replica", peer_slot),
        from_root(second_moment, "replica", peer_slot),
    )
    is_spare = position == spare_slot
    first_used = jnp.where(is_spare, received[0], first_moment)[0].astype(jnp.float32)
    second_used = jnp.where(is_spare, received[1], second_moment)[0].astype(jnp.float32)
    weights = anchor_new.astype(jnp.bfloat16)
    root = math.sqrt(weights.shape[1])
    cot_local = cotangent[0]
    tokens_part = lax.all_gather(activations, "shard", axis=1, tiled=True)[0]
    pre = (
        lax.dot_general(
            weights, tokens_part, (((1,), (1,)), ((), ())), preferred_element_type=jnp.float32
        )
        / root
    )
    grad_pre = (cot_local.astype(jnp.float32) * slope(pre)).astype(jnp.bfloat16)
    gradient = jnp.dot(grad_pre, tokens_part, preferred_element_type=jnp.float32) / root
    first = beta_one * first_used + (1.0 - beta_one) * gradient
    second = beta_two * second_used + (1.0 - beta_two) * gradient * gradient
    update = first / bias_one / (jnp.sqrt(second / bias_two) + adam_eps) + decay_rate * anchor_new
    return (anchor_new, momentum_new, update[None])


def solution(mesh):
    placed = (
        P("replica", "shard", None),
        P("shard", None),
        P("shard", None),
        P("replica", "shard", None),
        P("replica", "shard", None),
        P("replica", "shard", None),
        P("replica", "shard", None),
        P("shard"),
        P("shard"),
    )
    return jax.shard_map(
        local,
        mesh=mesh,
        in_specs=placed,
        out_specs=(P("shard", None), P("shard", None), P("replica", "shard", None)),
        check_vma=False,
    )
```

profile of v0, /device:TPU:1, one launch (start us, length us, event | category | flops | bytes accessed | tf_op | source)
XLA Modules:
  0.0 297.4 jit_solution(12718255101828199085)
XLA Ops:
  8.0 0.0 all-reduce.4.cloned.1.call-start
  8.7 2.7 fusion.6
  11.4 0.0 copy-start.2
  11.4 0.0 copy-start.3
  11.4 0.0 all-reduce.4.cloned.1.call-update
  11.4 0.0 all-reduce.6.cloned.1.call-start
  12.2 0.3 copy-done.2
  12.5 0.2 copy-done.3
  12.7 0.0 copy-start.4
  12.7 0.0 copy-start.1
  12.7 1.2 broadcast_select_fusion
  13.9 0.0 copy-start
  13.9 0.0 all-reduce.6.cloned.1.call-update
  13.9 0.0 all-gather.2.cloned.1.call-start
  14.0 0.0 copy-done.4
  14.0 0.7 copy.13
  14.7 0.0 all-gather.2.cloned.1.call-update
  14.7 0.0 copy-start.5
  14.7 66.7 %all-reduce.4.cloned.1.call-done = f32[80,4096]{1,0:T(8,128)} async-done(((f32[80,4096]{1,0:T(8,128)}), f32[80,4096]{1,0:T(8,128)}) %all-reduce.4.cloned.1.call-update) | async-done | bytes 1310736 | tf_op jit(solution)/shard_map/psum | solution.py:45
  81.4 0.0 copy-done.1
  81.4 0.0 copy-done
  81.4 3.2 %multiply_subtract_fusion = (f32[80,4096]{1,0:T(8,128)}, f32[80,4096]{1,0:T(8,128)}) fusion(f32[80,4096]{1,0:T(8,128)S(1)} %copy-done, f32[80,4096]{1,0:T(8,128)} %all-reduce.4.cloned.1.call-done, f32[80,4096]{1,0:T(8,128)S(1)} %copy-done.1), kind=kLoop, calls=%fused_computation.17 | loop fusion | flops 2293760 | bytes 6553600 | tf_op jit(solution)/shard_map/sub | solution.py:48
  84.6 67.7 %all-reduce.6.cloned.1.call-done = (bf16[1,80,4096]{2,1,0:T(8,128)(2,1)}, bf16[1,80,4096]{2,1,0:T(8,128)(2,1)}) async-done(((bf16[1,80,4096]{2,1,0:T(8,128)(2,1)}, bf16[1,80,4096]{2,1,0:T(8,128)(2,1)}), (bf16[1,80,4096]{2,1,0:T(8,128)(2,1)}, bf16[1,80,4096]{2,1,0:T(8,128)(2,1)})) %all-reduce.6.cloned.1.call-update) | async-done | bytes 1310736 | tf_op jit(solution)/shard_map/psum | solution.py:20
  152.3 112.8 %all-gather.2.cloned.1.call-done = bf16[1,768,4096]{2,0,1:T(2,128)(2,1)} async-done(((bf16[1,4,4096]{2,0,1:T(2,128)(2,1)}), bf16[1,768,4096]{2,0,1:T(2,128)(2,1)}) %all-gather.2.cloned.1.call-update) | async-done | bytes 6291472 | tf_op jit(solution)/shard_map/all_gather | solution.py:59
  265.1 0.0 copy-done.5
  265.1 24.9 %fusion.12 = f32[1,80,4096]{2,1,0:T(8,128)} fusion(f32[80,4096]{1,0:T(8,128)} %get-tuple-element.5, bf16[1,768,4096]{2,0,1:T(2,128)(2,1)} %all-gather.2.cloned.1.call-done, bf16[1,80,4096]{2,1,0:T(8,128)(2,1)} %get-tuple-element.3, bf16[1,80,4096]{2,1,0:T(8,128)(2,1)S(1)} %copy-done.2, bf16[1,80,4096]{2,1,0:T(8,128)(2,1)} %get-tuple-element.4, ...), kind=kOutput, calls=%fused_computation.14 | convolution fusion | flops 1013534720 | bytes 11657217 | tf_op jit(solution)/shard_map/dot_general | solution.py:67
Async XLA Ops:
  8.0 73.4 %all-reduce.4.cloned.1.call-start = ((), (), s32[]{:S(2)}) async-start(), calls=%async_computation | async-start | bytes 2621440 | tf_op jit(solution)/shard_map/psum | solution.py:45
  11.4 1.1 copy-start.2
  11.4 1.3 copy-start.3
  11.4 140.9 %all-reduce.6.cloned.1.call-start = ((), (), s32[]{:S(2)}) async-start(), calls=%async_computation.2 | async-start | bytes 2621440 | tf_op jit(solution)/shard_map/psum | solution.py:20
  12.7 1.3 copy-start.4
  12.7 68.7 %copy-start.1 = (f32[80,4096]{1,0:T(8,128)S(1)}, f32[80,4096]{1,0:T(8,128)}, u32[]{:S(2)}) copy-start(f32[80,4096]{1,0:T(8,128)} %param.11) | copy-start | bytes 3932164
  13.9 67.5 %copy-start = (f32[80,4096]{1,0:T(8,128)S(1)}, f32[80,4096]{1,0:T(8,128)}, u32[]{:S(2)}) copy-start(f32[80,4096]{1,0:T(8,128)} %param.10) | copy-start | bytes 3932164
  13.9 251.2 %all-gather.2.cloned.1.call-start = ((), (), s32[]{:S(2)}) async-start(), calls=%async_computation.1 | async-start | bytes 12648448 | tf_op jit(solution)/shard_map/all_gather | solution.py:59
  14.7 250.4 %copy-start.5 = (bf16[1,80,768]{2,1,0:T(8,128)(2,1)S(1)}, bf16[1,80,768]{2,1,0:T(8,128)(2,1)}, u32[]{:S(2)}) copy-start(bf16[1,80,768]{2,1,0:T(8,128)(2,1)} %param.15) | copy-start | bytes 368644
Sparse Core Ops, SparseCore 0:
  12.7 68.7 all-reduce.3
  84.7 67.5 all-reduce.5
Sparse Core Ops, SparseCore 1:
  20.0 245.1 all-gather.1
where the time goes:
time: 300 us; the launch traced here: 297 us
  waiting for transfers between devices  247 us (82%)
  matrix products  24.9 us (8%)
  between operations  16.9 us (6%)
  other arithmetic  7.07 us (2%)
    all_gather x1, waiting for transfers between devices, local(): tokens_part = lax.all_gather(activations, 'shard', axis=1, tiled=True)[0]  113 us
    psum x1, waiting for transfers between devices, from_root(): return lax.psum(block, axis)  67.7 us
    psum x1, waiting for transfers between devices, local(): summed = lax.psum(difference, 'replica')  66.7 us
    dot_general x1, matrix products, local(): jnp.dot(grad_pre, tokens_part, preferred_element_type=jnp.float32) / root  24.9 us
  transfers between devices with their start and end apart: 3, of which 3 were waited for; matrix products, arithmetic and copies ran while one was open for 2% of the time, Pallas kernels for 0%

commit v1 on v0

v1 whole, which is shorter than its diff:
```python
import functools

import jax
import jax.numpy as jnp
import numpy as np
from jax import lax
from jax.experimental import pallas as pl
from jax.experimental.pallas import tpu as pltpu
from jax.sharding import PartitionSpec as P

outer_rate = 0.7
nesterov_mu = 0.9
beta_one = 0.9
beta_two = 0.95
bias_one = 1.0 - 0.9**40
bias_two = 1.0 - 0.95**40
adam_eps = 1e-08
decay_rate = 0.1

NY, NZ = 8, 12
ROWS, D, TOK = 80, 4096, 768
HALF = D // 2
BR, BC = 16, 1024
PIECES = 4
ZP, YP = NZ // PIECES, NY // PIECES
f32, bf16 = jnp.float32, jnp.bfloat16


def slot(hops, way, ring):
    if hops == 0:
        return 0
    if 2 * hops == ring:
        return ring - 1
    return 2 * hops - 1 if way > 0 else 2 * hops


def offset_of(place, ring):
    if place == 0:
        return 0
    if place == ring - 1:
        return ring // 2
    hops = (place + 1) // 2
    return (ring - hops) if place % 2 else hops


GROUPS = [
    ("a", 0, 1, 0), ("a", 1, 1, 48), ("a", 2, 1, 96), ("b", 0, 1, 144), ("b", 1, 2, 176),
    ("a", 3, 1, 256), ("a", 4, 1, 304), ("b", 3, 2, 352), ("b", 5, 2, 416),
    ("a", 5, 1, 512), ("a", 6, 1, 560), ("b", 7, 2, 608),
    ("a", 7, 1, 768), ("b", 9, 2, 816), ("b", 11, 1, 880),
]
PADS = [(240, 256), (480, 512), (672, 768), (912, 1024)]


def token_table():
    table = np.zeros((8, 1024), np.int32)
    table[4] = 1
    for which, first, count, base in GROUPS:
        for row in range(first, first + count):
            for col in range(NZ if which == "a" else NY):
                yi, zi = (row, col) if which == "a" else (col, row)
                for t in range(4):
                    table[0, base] = offset_of(yi, NY)
                    table[1, base] = offset_of(zi, NZ)
                    table[2, base] = 0 if which == "a" else 1
                    table[3, base] = t
                    table[4, base] = 0
                    base += 1
    return table


def kernel(
    inner_ref, anchor_ref, momentum_ref, first_ref, second_ref, act_ref, cot_ref, spare_ref, peer_ref, table_ref,
    anchor_out, momentum_out, update_out,
    ga, gb, x, act_v, act_f, pb, an, mo, w, fm, mh, sel, rx, ca, cb, acc, cot, cotp, gp, perm, upd,
    load_sem, a1_s, a1_r, a2_s, a2_r, b1_s, b1_r, b2_s, b2_r, x_s, x_r, p_s, p_r, m_s, m_r, out_sem,
):
    r = lax.axis_index("replica")
    s = lax.axis_index("shard")
    core = r % 2
    xlo = r // 2
    y = s % NY
    z = (s // NY) % NZ
    xh = s // (NY * NZ)
    mate = r + 1 - 2 * core
    across = (r + 2) % 4
    far_mate = mate + 2 - 4 * xlo

    def at(rep, sh):
        return {"replica": rep, "shard": sh}

    y_to = {1: at(r, s - y + (y + 1) % NY), -1: at(r, s - y + (y + NY - 1) % NY)}
    z_to = {
        1: at(r, (xh * NZ + (z + 1) % NZ) * NY + y),
        -1: at(r, (xh * NZ + (z + NZ - 1) % NZ) * NY + y),
    }
    plane_to = at(r, (s + NY * NZ) % (2 * NY * NZ))
    mate_to = at(mate, s)
    across_to = at(across, s)

    loads = {}

    def load(name, i, src, dst):
        loads[name] = pltpu.make_async_copy(src, dst, load_sem.at[i])
        loads[name].start()

    load("act", 0, act_ref, act_v)
    load("inner", 1, inner_ref, pb.at[0])
    load("anchor", 2, anchor_ref, an)
    load("momentum", 3, momentum_ref, mo)
    load("first", 4, first_ref, fm.at[0])
    load("second", 5, second_ref, fm.at[1])
    load("cot", 6, cot_ref, cot)

    barrier = pltpu.get_barrier_semaphore()
    for to in (y_to[1], y_to[-1], z_to[1], z_to[-1], plane_to, mate_to, across_to):
        pl.semaphore_signal(barrier, inc=1, device_id=to, device_id_type=pl.DeviceIdType.MESH)

    loads["act"].wait()
    for q in range(4):
        act_f[4 * q : 4 * q + 4, :] = act_v[:, q * BC : (q + 1) * BC].astype(f32)
    ga[0:BR, :] = act_f[...].astype(bf16)

    pl.semaphore_wait(barrier, 7)

    made = {}

    def copy(key, src, dst, ss, rs, to):
        made[key] = pltpu.make_async_remote_copy(
            src_ref=src, dst_ref=dst, send_sem=ss, recv_sem=rs, device_id=to, device_id_type=pl.DeviceIdType.MESH
        )

    def ga_at(yi, zi, n):
        return ga.at[pl.ds((yi * NZ + zi) * BR, n * BR), :]

    def gb_at(zi, yi, n):
        return gb.at[pl.ds((zi * NY + yi) * BR, n * BR), :]

    def has(hops, way, ring, piece=None):
        if 2 * hops < ring:
            return True
        if 2 * hops > ring:
            return False
        if piece is None:
            return way > 0
        return (way > 0) == (piece < PIECES // 2)

    for way in (1, -1):
        for k in range(1, NZ // 2 + 1):
            a, b = slot(k - 1, way, NZ), slot(k, way, NZ)
            if has(k, way, NZ):
                copy(("a1", way, k), ga_at(0, a, 1), ga_at(0, b, 1), a1_s.at[b], a1_r.at[b], z_to[way])
            for q in range(PIECES):
                if has(k, way, NZ, q):
                    copy(("b2", way, k, q), gb_at(a, q * YP, YP), gb_at(b, q * YP, YP), b2_s.at[b, q], b2_r.at[b, q], z_to[way])
        for k in range(1, NY // 2 + 1):
            a, b = slot(k - 1, way, NY), slot(k, way, NY)
            if has(k, way, NY):
                copy(("b1", way, k), gb_at(0, a, 1), gb_at(0, b, 1), b1_s.at[b], b1_r.at[b], y_to[way])
            for q in range(PIECES):
                if has(k, way, NY, q):
                    copy(("a2", way, k, q), ga_at(a, q * ZP, ZP), ga_at(b, q * ZP, ZP), a2_s.at[b, q], a2_r.at[b, q], y_to[way])
    copy(("x",), ga_at(0, 0, 1), gb_at(0, 0, 1), x_s, x_r, plane_to)
    for j in range(5):
        rows = pl.ds(16 * j, 16)
        copy(("px", j), inner_ref.at[rows, :], pb.at[2, rows, :], p_s.at[0, j], p_r.at[0, j], across_to)
        copy(("pm", j), inner_ref.at[rows, :], pb.at[1, rows, :], p_s.at[1, j], p_r.at[1, j], mate_to)
        copy(("pf", j), pb.at[2, rows, :], pb.at[3, rows, :], p_s.at[2, j], p_r.at[2, j], mate_to)
    theirs = pl.ds(pl.multiple_of((1 - core) * HALF, HALF), HALF)
    for i, ref in enumerate((first_ref, second_ref)):
        copy(("mh", i), ref.at[:, theirs], mh.at[i], m_s.at[0, i], m_r.at[0, i], mate_to)
        copy(("mx", i), sel.at[i], rx.at[i], m_s.at[1, i], m_r.at[1, i], across_to)
        copy(("mc", i), ca.at[i], cb.at[i], m_s.at[2, i], m_r.at[2, i], mate_to)

    started, received = [], set()

    def start(*key):
        if key in made:
            made[key].start()
            assert key not in started
            started.append(key)

    def take(*key):
        if key in made:
            assert key in started and key not in received
            made[key].wait_recv()
            received.add(key)

    events = []

    def event(time, what):
        events.append((time, len(events), what))

    spare = spare_ref[0]
    peer = peer_ref[0]
    not_spare = [(spare != who).astype(f32) for who in (r, mate, across, far_mate)]

    def a1(k):
        for way in (1, -1):
            take("a1", way, k)
            start("a1", way, k + 1)

    def b1(k):
        for way in (1, -1):
            take("b1", way, k)
            start("b1", way, k + 1)

    def step(name, k, q):
        for way in (1, -1):
            if k:
                take(name, way, k, q)
            start(name, way, k + 1, q)

    def plane():
        take("x")
        start("b1", 1, 1)
        start("b1", -1, 1)

    a_in = {1: [0], 3: [1], 4: [2], 6: [3]}
    b_in = {1: [0], 2: [1], 3: [2], 4: [3]}
    for k in range(1, NZ // 2 + 1):
        event(2.2 * k, functools.partial(a1, k))
    event(2.9, plane)
    for k in range(1, NY // 2 + 1):
        event(2.9 + 2.2 * k, functools.partial(b1, k))
    for k, pieces in a_in.items():
        for q in pieces:
            event(2.2 * k + (0.8 if k == 1 else 0.01), functools.partial(step, "a2", 0, q))
    for k, pieces in b_in.items():
        for q in pieces:
            event(2.9 + 2.2 * k + 0.01, functools.partial(step, "b2", 0, q))

    def a2_time(k, q):
        return 6 + 12 * (k - 1) + 3 * ((q % 2 if 2 * k == NY else q) + 1) + 2

    def b2_time(k, q):
        return 10 + 8 * (k - 1) + 2 * ((q % 2 if 2 * k == NZ else q) + 1) + 2

    for q in range(PIECES):
        for k in range(1, NY // 2 + 1):
            event(a2_time(k, q), functools.partial(step, "a2", k, q))
        for k in range(1, NZ // 2 + 1):
            event(b2_time(k, q), functools.partial(step, "b2", k, q))

    def pass_on(j):
        take("px", j)
        start("pf", j)

    def outer(j):
        if j == 0:
            for name in ("inner", "anchor", "momentum"):
                loads[name].wait()
        take("pm", j)
        take("pf", j)
        rows = slice(16 * j, 16 * j + 16)

        @pl.loop(0, D // 512)
        def _(i):
            cols = pl.ds(pl.multiple_of(i * 512, 512), 512)
            a = an[rows, cols]
            total = jnp.zeros_like(a)
            for n in range(4):
                total = total + (a - pb[n, rows, cols].astype(f32)) * not_spare[n]
            average = total / 3.0
            fresh = nesterov_mu * mo[rows, cols] + average
            mo[rows, cols] = fresh
            a = a - outer_rate * (average + nesterov_mu * fresh)
            an[rows, cols] = a
            w[rows, cols] = a.astype(bf16)

    outs = {}

    def ship(name, i, src, dst):
        outs[name] = pltpu.make_async_copy(src, dst, out_sem.at[i])
        outs[name].start()

    for j in range(5):
        event(4 * (j + 1) + 2.5, functools.partial(pass_on, j))
        event(4 * (j + 1) + 5.5, functools.partial(outer, j))

    def ship_outer():
        ship("anchor", 0, an, anchor_out)
        ship("momentum", 1, mo, momentum_out)

    event(25.6, ship_outer)

    def choose():
        for name in ("first", "second"):
            loads[name].wait()
        for i in range(2):
            take("mh", i)

            @pl.loop(0, HALF // 512)
            def _(n):
                cols = pl.ds(pl.multiple_of(n * 512, 512), 512)
                high = pl.ds(pl.multiple_of(n * 512 + HALF, 512), 512)
                mine = jnp.where(core == 0, fm[i, :, cols].astype(f32), fm[i, :, high].astype(f32))
                sel[i, :, cols] = jnp.where(peer == mate, mh[i, :, cols].astype(f32), mine).astype(bf16)

            start("mx", i)

    def settle(i):
        take("mx", i)

        @pl.loop(0, HALF // 512)
        def _(n):
            cols = pl.ds(pl.multiple_of(n * 512, 512), 512)
            here = jnp.logical_or(peer == r, peer == mate)
            ca[i, :, cols] = jnp.where(here, sel[i, :, cols].astype(f32), rx[i, :, cols].astype(f32)).astype(bf16)

        start("mc", i)

    def adopt(i):
        take("mc", i)

        @pl.loop(0, HALF // 512)
        def _(n):
            for half in range(2):
                cols = pl.ds(pl.multiple_of(n * 512, 512), 512)
                dest = pl.ds(pl.multiple_of(n * 512 + half * HALF, 512), 512)
                new = jnp.where(core == half, ca[i, :, cols].astype(f32), cb[i, :, cols].astype(f32))
                fm[i, :, dest] = jnp.where(spare == r, new, fm[i, :, dest].astype(f32)).astype(bf16)

    event(4.0, choose)
    for i in range(2):
        event(34.2 + 10 * i, functools.partial(settle, i))
        event(37.2 + 10 * i, functools.partial(adopt, i))

    def prepare():
        for lo, hi in PADS:
            x[lo:hi, :] = jnp.zeros((hi - lo, D), bf16)
        for nth, blocks in enumerate((12, 16, 8)):
            n = blocks * BR
            out = lax.broadcasted_iota(jnp.int32, (n, n), 0)
            src = lax.broadcasted_iota(jnp.int32, (n, n), 1)
            quarter = (src % BR) // 4
            goal = quarter * (blocks * 4) + (src // BR) * 4 + src % 4
            perm[nth, 0:n, 0:n] = jnp.where(out == goal, 1.0, 0.0).astype(bf16)

    def reorder_cot(c):
        if c == 0:
            loads["cot"].wait()
        cols = slice(256 * c, 256 * c + 256)
        dy, dz, other, t, void = (table_ref[i : i + 1, cols] for i in range(5))
        yy = dy + y
        yy = jnp.where(yy >= NY, yy - NY, yy)
        zz = dz + z
        zz = jnp.where(zz >= NZ, zz - NZ, zz)
        hh = jnp.where(other == 1, 1 - xh, xh)
        token = ((hh * NZ + zz) * NY + yy) * 4 + t
        token = jnp.where(void == 1, -1, token)
        pick = lax.broadcasted_iota(jnp.int32, (TOK, 256), 0) == token
        cotp[:, cols] = jnp.dot(cot[...], jnp.where(pick, 1.0, 0.0).astype(bf16), preferred_element_type=f32)

    def arrange(which, first, count, base):
        buf, per = (ga, NZ) if which == "a" else (gb, NY)
        blocks = per * count
        n = blocks * BR
        nth = {12: 0, 16: 1, 8: 2}[blocks]

        for i in range(BC // 256):
            cols = slice(i * 256, i * 256 + 256)
            got = jnp.dot(
                perm[nth, 0:n, 0:n], buf[first * per * BR : first * per * BR + n, cols], preferred_element_type=f32
            ).astype(bf16)
            for q in range(4):
                x[base : base + blocks * 4, q * BC + i * 256 : q * BC + i * 256 + 256] = got[
                    q * blocks * 4 : (q + 1) * blocks * 4
                ]

    def slopes(c):
        rows = slice(256 * c, 256 * c + 256)
        pre = lax.dot_general(w[...], x[rows, :], (((1,), (1,)), ((), ())), preferred_element_type=f32) / 64.0
        sigma = jax.nn.sigmoid(pre)
        gp[...] = (cotp[:, rows] * (sigma * (1.0 + pre * (1.0 - sigma)))).astype(bf16)

    def gradient(c):
        rows = slice(256 * c, 256 * c + 256)
        slopes(c)

        @pl.loop(0, D // 512)
        def _(i):
            cols = pl.ds(pl.multiple_of(i * 512, 512), 512)
            part = jnp.dot(gp[...], x[rows, cols], preferred_element_type=f32)
            if c == 0:
                acc[:, cols] = part
            else:
                acc[:, cols] += part

    event(0.5, prepare)
    for c in range(4):
        event(1.0 + 1.1 * c + (0.15 if c else 0), functools.partial(reorder_cot, c))
    for which, first, count, base in GROUPS:
        last = first + count - 1
        if last == 0:
            ready = 2.2 * 6 + 0.1 if which == "a" else 2.9 + 2.2 * 4 + 0.1
        else:
            hops = (last + 1) // 2
            ready = (a2_time if which == "a" else b2_time)(hops, 3) + 0.1
        event(ready, functools.partial(arrange, which, first, count, base))
    event(27.0, functools.partial(gradient, 0))
    event(38.3, functools.partial(gradient, 1))
    event(46.3, functools.partial(gradient, 2))

    for way in (1, -1):
        start("a1", way, 1)
    start("x")
    for j in range(5):
        start("px", j)
    for i in range(2):
        start("mh", i)
    for j in range(5):
        start("pm", j)
    sent = 0
    for time, _, what in sorted(events, key=lambda e: e[:2]):
        what()

    c = 3
    rows = slice(256 * c, 256 * c + 256)
    slopes(c)

    @pl.loop(0, D // 256)
    def _(i):
        cols = pl.ds(pl.multiple_of(i * 256, 256), 256)
        g = (acc[:, cols] + jnp.dot(gp[...], x[rows, cols], preferred_element_type=f32)) * (1.0 / 64.0)
        first = beta_one * fm[0, :, cols].astype(f32) + (1.0 - beta_one) * g
        second = beta_two * fm[1, :, cols].astype(f32) + (1.0 - beta_two) * g * g
        upd[:, cols] = first / bias_one / (jnp.sqrt(second / bias_two) + adam_eps) + decay_rate * an[:, cols]

    ship("update", 2, upd, update_out)
    assert received == set(made) and len(started) == len(made)
    for key in started:
        made[key].wait_send()
    for name in outs:
        outs[name].wait()


def local(inner_params, anchor, momentum, first_moment, second_moment, activations, cotangent, spare_index, peer_index):
    hbm = pl.BlockSpec(memory_space=pltpu.MemorySpace.HBM)
    smem = pl.BlockSpec(memory_space=pltpu.SMEM)
    vmem = pl.BlockSpec(memory_space=pltpu.VMEM)
    dma = pltpu.SemaphoreType.DMA
    whole = jax.ShapeDtypeStruct((ROWS, D), f32)
    anchor_new, momentum_new, update = pl.pallas_call(
        kernel,
        out_shape=(whole, whole, whole),
        in_specs=[hbm] * 7 + [smem] * 2 + [vmem],
        out_specs=(hbm, hbm, hbm),
        scratch_shapes=[
            pltpu.VMEM((NY * NZ * BR, BC), bf16),
            pltpu.VMEM((NY * NZ * BR, BC), bf16),
            pltpu.VMEM((1024, D), bf16),
            pltpu.VMEM((4, D), bf16),
            pltpu.VMEM((BR, BC), f32),
            pltpu.VMEM((4, ROWS, D), bf16),
            pltpu.VMEM((ROWS, D), f32),
            pltpu.VMEM((ROWS, D), f32),
            pltpu.VMEM((ROWS, D), bf16),
            pltpu.VMEM((2, ROWS, D), bf16),
            pltpu.VMEM((2, ROWS, HALF), bf16),
            pltpu.VMEM((2, ROWS, HALF), bf16),
            pltpu.VMEM((2, ROWS, HALF), bf16),
            pltpu.VMEM((2, ROWS, HALF), bf16),
            pltpu.VMEM((2, ROWS, HALF), bf16),
            pltpu.VMEM((ROWS, D), f32),
            pltpu.VMEM((ROWS, TOK), bf16),
            pltpu.VMEM((ROWS, 1024), f32),
            pltpu.VMEM((ROWS, 256), bf16),
            pltpu.VMEM((3, 256, 256), bf16),
            pltpu.VMEM((ROWS, D), f32),
            dma((7,)),
            dma((NZ,)), dma((NZ,)),
            dma((NY, PIECES)), dma((NY, PIECES)),
            dma((NY,)), dma((NY,)),
            dma((NZ, PIECES)), dma((NZ, PIECES)),
            dma, dma,
            dma((3, 5)), dma((3, 5)),
            dma((3, 2)), dma((3, 2)),
            dma((3,)),
        ],
        compiler_params=pltpu.CompilerParams(
            collective_id=0, has_side_effects=True, vmem_limit_bytes=52 * 1024 * 1024
        ),
        cost_estimate=pl.CostEstimate(flops=2 * 2 * ROWS * D * TOK, bytes_accessed=9 << 20, transcendentals=ROWS * TOK),
    )(
        inner_params[0], anchor, momentum, first_moment[0], second_moment[0], activations[0], cotangent[0],
        spare_index, peer_index, jnp.asarray(token_table()),
    )
    return anchor_new, momentum_new, update[None]


def solution(mesh):
    placed = (
        P("replica", "shard", None),
        P("shard", None),
        P("shard", None),
        P("replica", "shard", None),
        P("replica", "shard", None),
        P("replica", "shard", None),
        P("replica", "shard", None),
        P("shard"),
        P("shard"),
    )
    return jax.shard_map(
        local,
        mesh=mesh,
        in_specs=placed,
        out_specs=(P("shard", None), P("shard", None), P("replica", "shard", None)),
        check_vma=False,
    )
```

time: 300 us -> 85.8 us (0.29)
  waiting for transfers between devices: 247 us -> 0 us
  Pallas kernels: 0 us -> 73.4 us
  matrix products: 24.9 us -> 0 us
  between operations: 16.9 us -> 1.96 us
  local copies, waits for them, and re-layouts: 1.17 us -> 10 us
  other arithmetic: 7.07 us -> 0 us
    psum x2 -> x0, waiting for transfers between devices: 134 us -> none  [the longest x1 67.7 us: from_root(): return lax.psum(block, axis)]
    all_gather x1 -> x0, waiting for transfers between devices: 113 us -> none  [local(): tokens_part = lax.all_gather(activations, 'shard', axis=1, tiled=True)[0]]
    pallas_call x0 -> x1, Pallas kernels: none -> 73.4 us  [local(): pl.pallas_call(kernel, out_shape=(whole, whole, whole), in_specs=[hbm] *...]
    dot_general x1 -> x0, matrix products: 24.9 us -> none  [local(): jnp.dot(grad_pre, tokens_part, preferred_element_type=jnp.float32) / root]
    unnamed x13 -> x17, local copies, waits for them, and re-layouts: 1.17 us -> 10 us
    sub x1 -> x0, other arithmetic: 3.18 us -> none  [local(): anchor_new = anchor - outer_rate * (average + nesterov_mu * momentum_new)]
  transfers between devices with their start and end apart: 3 -> 0, of which waited for: 3 -> 0; matrix products, arithmetic and copies ran while one was open for 2% -> 0% of each run, Pallas kernels for 0% -> 0%
where the time goes in v1:
time: 85.8 us; the launch traced here: 85.3 us
  Pallas kernels  73.4 us (86%)
  local copies, waits for them, and re-layouts  10 us (12%)
  between operations  1.96 us (2%)
    pallas_call x1, Pallas kernels, local(): pl.pallas_call(kernel, out_shape=(whole, whole, whole), in_specs=[hbm] *...  73.4 us
    unnamed x17, local copies, waits for them, and re-layouts  10 us

profile of v1, /device:TPU:1, one launch (start us, length us, event | category | flops | bytes accessed | tf_op | source)
XLA Modules:
  0.0 85.3 jit_solution(5272009603546775181)
XLA Ops:
  1.9 0.0 copy-start
  1.9 1.1 %copy-done = bf16[1,80,4096]{2,1,0:T(8,128)(2,1)S(1)} copy-done((bf16[1,80,4096]{2,1,0:T(8,128)(2,1)S(1)}, bf16[1,80,4096]{2,1,0:T(8,128)(2,1)}, u32[]{:S(2)}) %copy-start) | copy-done | bytes 655384
  3.0 0.0 copy-start.1
  3.0 1.1 %copy-done.1 = bf16[1,80,4096]{2,1,0:T(8,128)(2,1)S(1)} copy-done((bf16[1,80,4096]{2,1,0:T(8,128)(2,1)S(1)}, bf16[1,80,4096]{2,1,0:T(8,128)(2,1)}, u32[]{:S(2)}) %copy-start.1) | copy-done | bytes 655384
  4.1 0.0 copy-start.2
  4.1 0.9 %copy-done.2 = bf16[1,80,768]{2,1,0:T(8,128)(2,1)S(1)} copy-done((bf16[1,80,768]{2,1,0:T(8,128)(2,1)S(1)}, bf16[1,80,768]{2,1,0:T(8,128)(2,1)}, u32[]{:S(2)}) %copy-start.2) | copy-done | bytes 122904
  5.0 0.0 copy-start.3
  5.0 0.8 copy-done.3
  5.8 0.0 copy-start.4
  5.8 0.8 copy-done.4
  6.5 73.4 %shard_map.121 = (f32[80,4096]{1,0:T(8,128)}, f32[80,4096]{1,0:T(8,128)}, f32[80,4096]{1,0:T(8,128)}) custom-call(bf16[80,4096]{1,0:T(8,128)(2,1)S(1)} %bitcast.6, f32[80,4096]{1,0:T(8,128)} %anchor_ref.1, f32[80,4096]{1,0:T(8,128)} %momentum_ref.1, bf16[80,4096]{1,0:T(8,128)(2,1)S(1)} %bitcast.7, bf16[80,4096]{1,0:T(8,128)(2,1)} %bitcast.11, ...), custom_call_target="tpu_custom_call" | custom-call | flops 1006632960 | bytes 9437184 | tf_op jit(solution)/shard_map/pallas_call | solution.py:444
  79.9 0.0 copy-start.6
  79.9 2.6 %copy.18 = f32[80,4096]{1,0:T(8,128)} copy(f32[80,4096]{1,0:T(8,128)} %get-tuple-element.12) | data formatting | bytes 2621440
  82.5 0.0 copy-done.6
  82.5 0.0 copy-start.5
  82.5 1.1 %copy.19 = f32[80,4096]{1,0:T(8,128)} copy(f32[80,4096]{1,0:T(8,128)S(1)} %copy-done.6) | data formatting | bytes 2621440
  83.6 0.7 copy-done.5
  84.3 1.1 %copy.20 = f32[1,80,4096]{2,1,0:T(8,128)} copy(f32[1,80,4096]{2,1,0:T(8,128)S(1)} %bitcast.10) | data formatting | bytes 2621440
Async XLA Ops:
  1.9 1.1 %copy-start = (bf16[1,80,4096]{2,1,0:T(8,128)(2,1)S(1)}, bf16[1,80,4096]{2,1,0:T(8,128)(2,1)}, u32[]{:S(2)}) copy-start(bf16[1,80,4096]{2,1,0:T(8,128)(2,1)} %param.10) | copy-start | bytes 1966084
  3.0 1.1 %copy-start.1 = (bf16[1,80,4096]{2,1,0:T(8,128)(2,1)S(1)}, bf16[1,80,4096]{2,1,0:T(8,128)(2,1)}, u32[]{:S(2)}) copy-start(bf16[1,80,4096]{2,1,0:T(8,128)(2,1)} %param.13) | copy-start | bytes 1966084
  4.1 0.9 %copy-start.2 = (bf16[1,80,768]{2,1,0:T(8,128)(2,1)S(1)}, bf16[1,80,768]{2,1,0:T(8,128)(2,1)}, u32[]{:S(2)}) copy-start(bf16[1,80,768]{2,1,0:T(8,128)(2,1)} %param.16) | copy-start | bytes 368644
  5.0 0.8 copy-start.3
  5.8 0.8 copy-start.4
  79.9 2.6 %copy-start.6 = (f32[80,4096]{1,0:T(8,128)S(1)}, f32[80,4096]{1,0:T(8,128)}, u32[]{:S(2)}) copy-start(f32[80,4096]{1,0:T(8,128)} %get-tuple-element.13) | copy-start | bytes 3932164
  82.5 1.8 %copy-start.5 = (f32[80,4096]{1,0:T(8,128)S(1)}, f32[80,4096]{1,0:T(8,128)}, u32[]{:S(2)}) copy-start(f32[80,4096]{1,0:T(8,128)} %get-tuple-element.8) | copy-start | bytes 3932164

commit v2 on v1

--- a/solution.py
+++ b/solution.py
@@ -70,9 +70,9 @@
 
 
 def kernel(
-    inner_ref, anchor_ref, momentum_ref, first_ref, second_ref, act_ref, cot_ref, spare_ref, peer_ref, table_ref,
-    anchor_out, momentum_out, update_out,
-    ga, gb, x, act_v, act_f, pb, an, mo, w, fm, mh, sel, rx, ca, cb, acc, cot, cotp, gp, perm, upd,
+    inner_ref, anchor_ref, momentum_ref, first_ref, second_ref, act_ref, cot_ref, spare_in, peer_in, table_in,
+    average_out, first_out, second_out, gradient_out,
+    ga, gb, x, act_v, act_f, pb, an, mo, w, fm, mh, sel, rx, ca, cb, acc, cot, cotp, gp, perm, table_ref, spare_ref, peer_ref,
     load_sem, a1_s, a1_r, a2_s, a2_r, b1_s, b1_r, b2_s, b2_r, x_s, x_r, p_s, p_r, m_s, m_r, out_sem,
 ):
     r = lax.axis_index("replica")
@@ -111,6 +111,9 @@
     load("first", 4, first_ref, fm.at[0])
     load("second", 5, second_ref, fm.at[1])
     load("cot", 6, cot_ref, cot)
+    load("table", 7, table_in, table_ref)
+    load("spare", 8, spare_in, spare_ref)
+    load("peer", 9, peer_in, peer_ref)
 
     barrier = pltpu.get_barrier_semaphore()
     for to in (y_to[1], y_to[-1], z_to[1], z_to[-1], plane_to, mate_to, across_to):
@@ -191,6 +194,8 @@
     def event(time, what):
         events.append((time, len(events), what))
 
+    loads["spare"].wait()
+    loads["peer"].wait()
     spare = spare_ref[0]
     peer = peer_ref[0]
     not_spare = [(spare != who).astype(f32) for who in (r, mate, across, far_mate)]
@@ -263,10 +268,8 @@
                 total = total + (a - pb[n, rows, cols].astype(f32)) * not_spare[n]
             average = total / 3.0
             fresh = nesterov_mu * mo[rows, cols] + average
-            mo[rows, cols] = fresh
-            a = a - outer_rate * (average + nesterov_mu * fresh)
-            an[rows, cols] = a
-            w[rows, cols] = a.astype(bf16)
+            an[rows, cols] = average
+            w[rows, cols] = (a - outer_rate * (average + nesterov_mu * fresh)).astype(bf16)
 
     outs = {}
 
@@ -278,11 +281,7 @@
         event(4 * (j + 1) + 2.5, functools.partial(pass_on, j))
         event(4 * (j + 1) + 5.5, functools.partial(outer, j))
 
-    def ship_outer():
-        ship("anchor", 0, an, anchor_out)
-        ship("momentum", 1, mo, momentum_out)
-
-    event(25.6, ship_outer)
+    event(25.6, functools.partial(ship, "average", 0, an, average_out))
 
     def choose():
         for name in ("first", "second"):
@@ -325,6 +324,7 @@
     for i in range(2):
         event(34.2 + 10 * i, functools.partial(settle, i))
         event(37.2 + 10 * i, functools.partial(adopt, i))
+        event(37.2 + 10 * i, functools.partial(ship, ("first", "second")[i], i + 1, fm.at[i], (first_out, second_out)[i]))
 
     def prepare():
         for lo, hi in PADS:
@@ -340,6 +340,7 @@
     def reorder_cot(c):
         if c == 0:
             loads["cot"].wait()
+            loads["table"].wait()
         cols = slice(256 * c, 256 * c + 256)
         dy, dz, other, t, void = (table_ref[i : i + 1, cols] for i in range(5))
         yy = dy + y
@@ -411,23 +412,17 @@
         start("mh", i)
     for j in range(5):
         start("pm", j)
-    sent = 0
-    for time, _, what in sorted(events, key=lambda e: e[:2]):
+    for _, _, what in sorted(events, key=lambda e: e[:2]):
         what()
 
-    c = 3
-    rows = slice(256 * c, 256 * c + 256)
-    slopes(c)
-
-    @pl.loop(0, D // 256)
-    def _(i):
-        cols = pl.ds(pl.multiple_of(i * 256, 256), 256)
-        g = (acc[:, cols] + jnp.dot(gp[...], x[rows, cols], preferred_element_type=f32)) * (1.0 / 64.0)
-        first = beta_one * fm[0, :, cols].astype(f32) + (1.0 - beta_one) * g
-        second = beta_two * fm[1, :, cols].astype(f32) + (1.0 - beta_two) * g * g
-        upd[:, cols] = first / bias_one / (jnp.sqrt(second / bias_two) + adam_eps) + decay_rate * an[:, cols]
-
-    ship("update", 2, upd, update_out)
+    slopes(3)
+    for i in range(8):
+        cols = slice(512 * i, 512 * i + 512)
+        acc[:, cols] += jnp.dot(gp[...], x[768:1024, cols], preferred_element_type=f32)
+        if i % 2:
+            part = slice(512 * (i - 1), 512 * (i + 1))
+            ship(("gradient", i // 2), 3 + i // 2, acc.at[:, part], gradient_out.at[:, part])
+
     assert received == set(made) and len(started) == len(made)
     for key in started:
         made[key].wait_send()
@@ -437,15 +432,14 @@
 
 def local(inner_params, anchor, momentum, first_moment, second_moment, activations, cotangent, spare_index, peer_index):
     hbm = pl.BlockSpec(memory_space=pltpu.MemorySpace.HBM)
-    smem = pl.BlockSpec(memory_space=pltpu.SMEM)
-    vmem = pl.BlockSpec(memory_space=pltpu.VMEM)
     dma = pltpu.SemaphoreType.DMA
     whole = jax.ShapeDtypeStruct((ROWS, D), f32)
-    anchor_new, momentum_new, update = pl.pallas_call(
+    half = jax.ShapeDtypeStruct((ROWS, D), bf16)
+    average, first_used, second_used, gradient = pl.pallas_call(
         kernel,
-        out_shape=(whole, whole, whole),
-        in_specs=[hbm] * 7 + [smem] * 2 + [vmem],
-        out_specs=(hbm, hbm, hbm),
+        out_shape=(whole, half, half, whole),
+        in_specs=[hbm] * 10,
+        out_specs=(hbm,) * 4,
         scratch_shapes=[
             pltpu.VMEM((NY * NZ * BR, BC), bf16),
             pltpu.VMEM((NY * NZ * BR, BC), bf16),
@@ -467,8 +461,10 @@
             pltpu.VMEM((ROWS, 1024), f32),
             pltpu.VMEM((ROWS, 256), bf16),
             pltpu.VMEM((3, 256, 256), bf16),
-            pltpu.VMEM((ROWS, D), f32),
-            dma((7,)),
+            pltpu.VMEM((8, 1024), jnp.int32),
+            pltpu.SMEM((1,), jnp.int32),
+            pltpu.SMEM((1,), jnp.int32),
+            dma((10,)),
             dma((NZ,)), dma((NZ,)),
             dma((NY, PIECES)), dma((NY, PIECES)),
             dma((NY,)), dma((NY,)),
@@ -476,16 +472,22 @@
             dma, dma,
             dma((3, 5)), dma((3, 5)),
             dma((3, 2)), dma((3, 2)),
-            dma((3,)),
+            dma((7,)),
         ],
         compiler_params=pltpu.CompilerParams(
-            collective_id=0, has_side_effects=True, vmem_limit_bytes=52 * 1024 * 1024
+            collective_id=0, has_side_effects=True, vmem_limit_bytes=61 * 1024 * 1024
         ),
         cost_estimate=pl.CostEstimate(flops=2 * 2 * ROWS * D * TOK, bytes_accessed=9 << 20, transcendentals=ROWS * TOK),
     )(
         inner_params[0], anchor, momentum, first_moment[0], second_moment[0], activations[0], cotangent[0],
         spare_index, peer_index, jnp.asarray(token_table()),
     )
+    momentum_new = nesterov_mu * momentum + average
+    anchor_new = anchor - outer_rate * (average + nesterov_mu * momentum_new)
+    gradient = gradient * (1.0 / 64.0)
+    first = beta_one * first_used.astype(f32) + (1.0 - beta_one) * gradient
+    second = beta_two * second_used.astype(f32) + (1.0 - beta_two) * gradient * gradient
+    update = first / bias_one / (jnp.sqrt(second / bias_two) + adam_eps) + decay_rate * anchor_new
     return anchor_new, momentum_new, update[None]
 
 

time: 85.8 us -> 76.6 us (0.89)
  local copies, waits for them, and re-layouts: 10 us -> 0.01 us
  other arithmetic: 0 us -> 4.68 us
  Pallas kernels: 73.4 us -> 69.8 us
    unnamed x17 -> x4, local copies, waits for them, and re-layouts: 10 us -> 0.01 us
    broadcast_in_dim x0 -> x1, other arithmetic: none -> 4.68 us  [local(): return (anchor_new, momentum_new, update[None])]
    pallas_call x1, Pallas kernels: 73.4 us -> 69.8 us  [local(): pl.pallas_call(kernel, out_shape=(whole, half, half, whole), in_specs=[hb...]
where the time goes in v2:
time: 76.6 us; the launch traced here: 76.5 us
  Pallas kernels  69.8 us (91%)
  other arithmetic  4.68 us (6%)
  between operations  1.96 us (3%)
    pallas_call x1, Pallas kernels, local(): pl.pallas_call(kernel, out_shape=(whole, half, half, whole), in_specs=[hb...  69.8 us
    broadcast_in_dim x1, other arithmetic, local(): return (anchor_new, momentum_new, update[None])  4.68 us

profile of v2, /device:TPU:1, one launch (start us, length us, event | category | flops | bytes accessed | tf_op | source)
XLA Modules:
  0.0 76.5 jit_solution(8793556168250388414)
XLA Ops:
  1.9 0.0 copy-start
  1.9 0.0 copy-start.1
  1.9 69.8 %shard_map.121 = (f32[80,4096]{1,0:T(8,128)}, bf16[80,4096]{1,0:T(8,128)(2,1)}, bf16[80,4096]{1,0:T(8,128)(2,1)}, f32[80,4096]{1,0:T(8,128)}) custom-call(bf16[80,4096]{1,0:T(8,128)(2,1)} %bitcast.7, f32[80,4096]{1,0:T(8,128)} %anchor_ref.1, f32[80,4096]{1,0:T(8,128)} %momentum_ref.1, bf16[80,4096]{1,0:T(8,128)(2,1)} %bitcast.8, bf16[80,4096]{1,0:T(8,128)(2,1)} %bitcast.9, ...), custom_call_target="tpu_custom_call" | custom-call | flops 1006632960 | bytes 9437184 | tf_op jit(solution)/shard_map/pallas_call | solution.py:438
  71.8 0.0 copy-done
  71.8 0.0 copy-done.1
  71.8 4.7 %add_bitcast_fusion = (f32[1,80,4096]{2,1,0:T(8,128)}, f32[80,4096]{1,0:T(8,128)}, f32[80,4096]{1,0:T(8,128)}) fusion(f32[80,4096]{1,0:T(8,128)} %get-tuple-element.9, bf16[80,4096]{1,0:T(8,128)(2,1)} %get-tuple-element.10, bf16[80,4096]{1,0:T(8,128)(2,1)} %get-tuple-element.8, f32[80,4096]{1,0:T(8,128)S(1)} %copy-done, f32[80,4096]{1,0:T(8,128)} %get-tuple-element.7, ...), kind=kLoop, calls=%fused_computation | loop fusion | flops 7208960 | bytes 10485760 | tf_op jit(solution)/shard_map/broadcast_in_dim | solution.py:491
Async XLA Ops:
  1.9 69.9 %copy-start = (f32[80,4096]{1,0:T(8,128)S(1)}, f32[80,4096]{1,0:T(8,128)}, u32[]{:S(2)}) copy-start(f32[80,4096]{1,0:T(8,128)} %anchor_ref.1) | copy-start | bytes 3932164
  1.9 69.9 %copy-start.1 = (f32[80,4096]{1,0:T(8,128)S(1)}, f32[80,4096]{1,0:T(8,128)}, u32[]{:S(2)}) copy-start(f32[80,4096]{1,0:T(8,128)} %momentum_ref.1) | copy-start | bytes 3932164

commit v3 on v2

--- a/solution.py
+++ b/solution.py
@@ -50,6 +50,9 @@
     ("a", 7, 1, 768), ("b", 9, 2, 816), ("b", 11, 1, 880),
 ]
 PADS = [(240, 256), (480, 512), (672, 768), (912, 1024)]
+
+
+FROM_TWIN = [(0, 9), (0, 10), (0, 11), (1, 9), (1, 10), (1, 11), (2, 11), (3, 11)]
 
 
 def token_table():
@@ -73,7 +76,7 @@
     inner_ref, anchor_ref, momentum_ref, first_ref, second_ref, act_ref, cot_ref, spare_in, peer_in, table_in,
     average_out, first_out, second_out, gradient_out,
     ga, gb, x, act_v, act_f, pb, an, mo, w, fm, mh, sel, rx, ca, cb, acc, cot, cotp, gp, perm, table_ref, spare_ref, peer_ref,
-    load_sem, a1_s, a1_r, a2_s, a2_r, b1_s, b1_r, b2_s, b2_r, x_s, x_r, p_s, p_r, m_s, m_r, out_sem,
+    load_sem, a1_s, a1_r, a2_s, a2_r, b1_s, b1_r, b2_s, b2_r, x_s, x_r, xb_s, xb_r, p_s, p_r, m_s, m_r, out_sem,
 ):
     r = lax.axis_index("replica")
     s = lax.axis_index("shard")
@@ -148,13 +151,20 @@
             return way > 0
         return (way > 0) == (piece < PIECES // 2)
 
+    def by_ring(k, way, q):
+        if 2 * k < NZ:
+            return (k, q) != (NZ // 2 - 1, 0)
+        return q == (2 if way > 0 else 3)
+
+    for i, (yi, zi) in enumerate(FROM_TWIN):
+        copy(("xb", i), ga_at(yi, zi, 1), gb_at(zi, yi, 1), xb_s.at[i], xb_r.at[i], plane_to)
     for way in (1, -1):
         for k in range(1, NZ // 2 + 1):
             a, b = slot(k - 1, way, NZ), slot(k, way, NZ)
             if has(k, way, NZ):
                 copy(("a1", way, k), ga_at(0, a, 1), ga_at(0, b, 1), a1_s.at[b], a1_r.at[b], z_to[way])
             for q in range(PIECES):
-                if has(k, way, NZ, q):
+                if by_ring(k, way, q):
                     copy(("b2", way, k, q), gb_at(a, q * YP, YP), gb_at(b, q * YP, YP), b2_s.at[b, q], b2_r.at[b, q], z_to[way])
         for k in range(1, NY // 2 + 1):
             a, b = slot(k - 1, way, NY), slot(k, way, NY)
@@ -175,7 +185,13 @@
         copy(("mx", i), sel.at[i], rx.at[i], m_s.at[1, i], m_r.at[1, i], across_to)
         copy(("mc", i), ca.at[i], cb.at[i], m_s.at[2, i], m_r.at[2, i], mate_to)
 
-    started, received = [], set()
+    started, received, settled = [], set(), set()
+
+    def clear():
+        for key in started:
+            if key in received and key not in settled:
+                made[key].wait_send()
+                settled.add(key)
 
     def start(*key):
         if key in made:
@@ -247,6 +263,19 @@
         for k in range(1, NZ // 2 + 1):
             event(b2_time(k, q), functools.partial(step, "b2", k, q))
 
+    def twin(act, *which):
+        for i in which:
+            act("xb", i)
+
+    event(11.005, functools.partial(twin, start, 0, 1))
+    event(13.205, functools.partial(twin, start, 2))
+    event(20.001, functools.partial(twin, start, 3, 4, 5, 6))
+    event(32.001, functools.partial(twin, start, 7))
+    event(52.05, functools.partial(twin, take, 0, 1, 3, 4))
+    event(56.05, functools.partial(twin, take, 2, 5, 6, 7))
+    for time in (24.5, 36.5, 48.5, 53.6):
+        event(time, clear)
+
     def pass_on(j):
         take("px", j)
         start("pf", j)
@@ -322,9 +351,9 @@
 
     event(4.0, choose)
     for i in range(2):
-        event(34.2 + 10 * i, functools.partial(settle, i))
-        event(37.2 + 10 * i, functools.partial(adopt, i))
-        event(37.2 + 10 * i, functools.partial(ship, ("first", "second")[i], i + 1, fm.at[i], (first_out, second_out)[i]))
+        event(36.2 + 14 * i, functools.partial(settle, i))
+        event(39.2 + 14 * i, functools.partial(adopt, i))
+        event(39.2 + 14 * i, functools.partial(ship, ("first", "second")[i], i + 1, fm.at[i], (first_out, second_out)[i]))
 
     def prepare():
         for lo, hi in PADS:
@@ -424,8 +453,8 @@
             ship(("gradient", i // 2), 3 + i // 2, acc.at[:, part], gradient_out.at[:, part])
 
     assert received == set(made) and len(started) == len(made)
-    for key in started:
-        made[key].wait_send()
+    clear()
+    assert len(settled) == len(made)
     for name in outs:
         outs[name].wait()
 
@@ -470,6 +499,7 @@
             dma((NY,)), dma((NY,)),
             dma((NZ, PIECES)), dma((NZ, PIECES)),
             dma, dma,
+            dma((8,)), dma((8,)),
             dma((3, 5)), dma((3, 5)),
             dma((3, 2)), dma((3, 2)),
             dma((7,)),
@@ -487,7 +517,7 @@
     gradient = gradient * (1.0 / 64.0)
     first = beta_one * first_used.astype(f32) + (1.0 - beta_one) * gradient
     second = beta_two * second_used.astype(f32) + (1.0 - beta_two) * gradient * gradient
-    update = first / bias_one / (jnp.sqrt(second / bias_two) + adam_eps) + decay_rate * anchor_new
+    update = first * (1.0 / bias_one) / (jnp.sqrt(second * (1.0 / bias_two)) + adam_eps) + decay_rate * anchor_new
     return anchor_new, momentum_new, update[None]
 
 

time: 76.6 us -> 75.6 us (0.987)
  Pallas kernels: 69.8 us -> 68.8 us
    pallas_call x1, Pallas kernels: 69.8 us -> 68.8 us  [local(): pl.pallas_call(kernel, out_shape=(whole, half, half, whole), in_specs=[hb...]
where the time goes in v3:
time: 75.6 us; the launch traced here: 75.4 us
  Pallas kernels  68.8 us (91%)
  other arithmetic  4.68 us (6%)
  between operations  1.96 us (3%)
    pallas_call x1, Pallas kernels, local(): pl.pallas_call(kernel, out_shape=(whole, half, half, whole), in_specs=[hb...  68.8 us
    broadcast_in_dim x1, other arithmetic, local(): return (anchor_new, momentum_new, update[None])  4.68 us

profile of v3, /device:TPU:1, one launch (start us, length us, event | category | flops | bytes accessed | tf_op | source)
XLA Modules:
  0.0 75.4 jit_solution(1891226056295470726)
XLA Ops:
  1.9 0.0 copy-start
  1.9 0.0 copy-start.1
  1.9 68.8 %shard_map.121 = (f32[80,4096]{1,0:T(8,128)}, bf16[80,4096]{1,0:T(8,128)(2,1)}, bf16[80,4096]{1,0:T(8,128)(2,1)}, f32[80,4096]{1,0:T(8,128)}) custom-call(bf16[80,4096]{1,0:T(8,128)(2,1)} %bitcast.7, f32[80,4096]{1,0:T(8,128)} %anchor_ref.1, f32[80,4096]{1,0:T(8,128)} %momentum_ref.1, bf16[80,4096]{1,0:T(8,128)(2,1)} %bitcast.8, bf16[80,4096]{1,0:T(8,128)(2,1)} %bitcast.9, ...), custom_call_target="tpu_custom_call" | custom-call | flops 1006632960 | bytes 9437184 | tf_op jit(solution)/shard_map/pallas_call | solution.py:467
  70.7 0.0 copy-done
  70.7 0.0 copy-done.1
  70.7 4.7 %add_bitcast_fusion = (f32[1,80,4096]{2,1,0:T(8,128)}, f32[80,4096]{1,0:T(8,128)}, f32[80,4096]{1,0:T(8,128)}) fusion(f32[80,4096]{1,0:T(8,128)} %get-tuple-element.9, bf16[80,4096]{1,0:T(8,128)(2,1)} %get-tuple-element.10, bf16[80,4096]{1,0:T(8,128)(2,1)} %get-tuple-element.8, f32[80,4096]{1,0:T(8,128)S(1)} %copy-done, f32[80,4096]{1,0:T(8,128)} %get-tuple-element.7, ...), kind=kLoop, calls=%fused_computation | loop fusion | flops 7208960 | bytes 10485760 | tf_op jit(solution)/shard_map/broadcast_in_dim | solution.py:521
Async XLA Ops:
  1.9 68.8 %copy-start = (f32[80,4096]{1,0:T(8,128)S(1)}, f32[80,4096]{1,0:T(8,128)}, u32[]{:S(2)}) copy-start(f32[80,4096]{1,0:T(8,128)} %anchor_ref.1) | copy-start | bytes 3932164
  1.9 68.8 %copy-start.1 = (f32[80,4096]{1,0:T(8,128)S(1)}, f32[80,4096]{1,0:T(8,128)}, u32[]{:S(2)}) copy-start(f32[80,4096]{1,0:T(8,128)} %momentum_ref.1) | copy-start | bytes 3932164
